TPU v7x, 128 devices: a whole 4x4x4 slice. The times are simulated.
128 devices in a mesh: section: 16 (over x_lo, y, core), island: 8 (over x_hi, z).
Axes of the slice: x: 4 (x_hi: 2, x_lo: 2; x = x_hi * 2 + x_lo), y: 4, z: 4, core: 2. Of those that a mesh axis runs over, the one named last changes fastest.
Arguments:
- inputs: bfloat16 [8, 512, 16384], P('island', None, 'section'), may hold values from -6 to 6
- gate_pre: bfloat16 [8, 512, 3328], P('island', 'section'), may hold values from -6 to 6
- up_cot: bfloat16 [8, 512, 3328], P('island', 'section'), may hold values from -6 to 6
- weights: bfloat16 [8, 16384, 3328], P('island', 'section'), may hold values from -0.0625 to 0.0625
- outer: float32 [16384, 3328], P(('section', 'island')), may hold values from -0.6 to 0.6
- momentum: float32 [16384, 3328], P(('section', 'island')), may hold values from -0.6 to 0.6
Outputs:
- input_grad: bfloat16 [8, 512, 16384], P('island', None, 'section')
- gate_grad: bfloat16 [8, 512, 3328], P('island', 'section')
- new_weights: bfloat16 [16384, 3328], P('section')
- new_outer: float32 [16384, 3328], P(('section', 'island'))
- new_momentum: float32 [16384, 3328], P(('section', 'island'))
All inputs are finite; a program needn't handle non-finite values.
Results may differ from a plain program's by a relative error of at most 0.01.
Values may be sent and summed in bfloat16 or wider, within the bound.
A program may use at most 128 MiB of HBM per device.

v0:
```python
import jax
import jax.numpy as jnp
from jax import lax
from jax.sharding import PartitionSpec as P

inner_rate = 0.0005
outer_rate = 0.7
nesterov_mu = 0.9


def contract_rows(left_rows, right_rows):
    return lax.dot_general(
        left_rows, right_rows, (((0,), (0,)), ((), ())), preferred_element_type=jnp.float32
    )


def gated_grad(shard_piece):
    gate_piece = shard_piece[0].astype(jnp.float32)
    return (shard_piece[1].astype(jnp.float32) * gate_piece * jax.nn.sigmoid(gate_piece)).astype(
        jnp.bfloat16
    )


def local(inputs, gate_pre, up_cot, weights, outer, momentum):
    features = inputs[0]
    gate_mine = gate_pre[0]
    cot_mine = up_cot[0]
    weight = weights[0]
    row_block = features
    up_mine = lax.psum_scatter(
        jnp.dot(row_block, weight, preferred_element_type=jnp.float32),
        "section",
        scatter_dimension=0,
        tiled=True,
    )
    gate_full = gate_mine.astype(jnp.float32)
    gate_sigma = jax.nn.sigmoid(gate_full)
    gate_grad = (
        cot_mine.astype(jnp.float32) * up_mine * gate_sigma * (1.0 + gate_full * (1.0 - gate_sigma))
    ).astype(jnp.bfloat16)
    d_up = gated_grad(
        (
            lax.all_gather(gate_mine, "section", axis=0, tiled=True),
            lax.all_gather(cot_mine, "section", axis=0, tiled=True),
        )
    )
    row_block = features
    weight_grad = contract_rows(row_block, d_up)
    pulled_back = lax.dot_general(
        d_up, weight, (((1,), (1,)), ((), ())), preferred_element_type=jnp.float32
    )
    input_grad = pulled_back.astype(jnp.bfloat16)
    inner_block = weight.astype(jnp.float32) - inner_rate * weight_grad
    summed = lax.psum_scatter(
        inner_block.astype(jnp.bfloat16), "island", scatter_dimension=0, tiled=True
    ).astype(jnp.float32)
    mean_inner = summed / lax.axis_size("island")
    delta_rows = outer - mean_inner
    moment = nesterov_mu * momentum + delta_rows
    updated = outer - outer_rate * (delta_rows + nesterov_mu * moment)
    gathered = lax.all_gather(updated.astype(jnp.bfloat16), "island", axis=0, tiled=True)
    return (input_grad[None], gate_grad[None], gathered, updated, moment)


def solution(mesh):
    placed = (
        P("island", None, "section"),
        P("island", "section", None),
        P("island", "section", None),
        P("island", "section", None),
        P(("section", "island"), None),
        P(("section", "island"), None),
    )
    return jax.shard_map(
        local,
        mesh=mesh,
        in_specs=placed,
        out_specs=(
            P("island", None, "section"),
            P("island", "section", None),
            P("section", None),
            P(("section", "island"), None),
            P(("section", "island"), None),
        ),
        check_vma=False,
    )
```

profile of v0, /device:TPU:0, one launch (start us, length us, event | category | flops | bytes accessed | tf_op | source)
XLA Modules:
  0.0 401.7 jit_solution(8050078827049434846)
XLA Ops:
  7.2 0.0 copy-start
  7.2 0.0 all-gather.10.cloned.1.call-start
  7.2 0.7 all-gather.10.cloned.1.call-update
  7.9 0.0 all-gather.8.cloned.1.call-start
  8.0 0.7 all-gather.8.cloned.1.call-update
  8.7 0.0 reduce-scatter.7.cloned.1.call-start
  8.7 9.9 %copy.18 = bf16[1,1024,3328]{1,2,0:T(8,128)(2,1)} copy(bf16[1,1024,3328]{2,1,0:T(8,128)(2,1)} %param.9) | data formatting | bytes 13631488 | tf_op args[3]
  18.7 29.9 %all-gather.10.cloned.1.call-done = bf16[1,512,3328]{2,1,0:T(8,128)(2,1)} async-done(((bf16[1,32,3328]{2,1,0:T(8,128)(2,1)}), bf16[1,512,3328]{2,1,0:T(8,128)(2,1)}) %all-gather.10.cloned.1.call-update) | async-done | bytes 3407888 | tf_op jit(solution)/shard_map/all_gather | solution.py:43
  48.5 38.1 %all-gather.8.cloned.1.call-done = bf16[1,512,3328]{2,1,0:T(8,128)(2,1)} async-done(((bf16[1,32,3328]{2,1,0:T(8,128)(2,1)}), bf16[1,512,3328]{2,1,0:T(8,128)(2,1)}) %all-gather.8.cloned.1.call-update) | async-done | bytes 3407888 | tf_op jit(solution)/shard_map/all_gather | solution.py:44
  86.6 0.0 copy-done
  86.6 13.1 %fusion = bf16[1024,3328]{0,1:T(8,128)(2,1)} fusion(bf16[1,1024,3328]{1,2,0:T(8,128)(2,1)} %copy.18, bf16[1,512,1024]{2,1,0:T(8,128)(2,1)S(1)} %copy-done, bf16[1,512,3328]{2,1,0:T(8,128)(2,1)} %all-gather.10.cloned.1.call-done, bf16[1,512,3328]{2,1,0:T(8,128)(2,1)} %all-gather.8.cloned.1.call-done), kind=kOutput, calls=%fused_computation.1 | convolution fusion | flops 3516923904 | bytes 21495808 | tf_op jit(solution)/shard_map/dot_general | solution.py:12
  99.7 9.9 %copy.25 = bf16[1024,3328]{1,0:T(8,128)(2,1)} copy(bf16[1024,3328]{0,1:T(8,128)(2,1)} %fusion) | data formatting | bytes 13631488
  109.7 0.0 reduce-scatter.7.cloned.1.call-update
  109.7 0.0 reduce-scatter.5.cloned.1.call-start
  109.7 8.6 %fusion.5 = f32[512,3328]{1,0:T(8,128)} fusion(bf16[1,1024,3328]{2,1,0:T(8,128)(2,1)} %param.9, bf16[1,512,1024]{2,1,0:T(8,128)(2,1)S(1)} %copy-done), kind=kOutput, calls=%fused_computation.8 | convolution fusion | flops 3489660928 | bytes 14680064 | tf_op jit(solution)/shard_map/dot_general | solution.py:31
  118.3 0.0 copy-start.2
  118.3 0.0 reduce-scatter.5.cloned.1.call-update
  118.3 0.2 all-gather.6.cloned.1.call-start
  118.6 1.7 copy-done.2
  120.2 1.6 copy.21
  121.9 2.7 copy.20
  124.5 89.0 %reduce-scatter.7.cloned.1.call-done = bf16[128,3328]{1,0:T(8,128)(2,1)} async-done(((bf16[1024,3328]{1,0:T(8,128)(2,1)}), bf16[128,3328]{1,0:T(8,128)(2,1)}) %reduce-scatter.7.cloned.1.call-update) | async-done | bytes 851984
  213.6 1.5 copy.26
  215.1 4.0 fusion.34
  219.1 0.0 all-gather.6.cloned.1.call-update
  219.1 0.0 copy-start.3
  219.2 0.0 copy-start.4
  219.2 10.3 %fusion.17 = bf16[1,512,1024]{2,1,0:T(8,128)(2,1)} fusion(bf16[1,1024,3328]{2,1,0:T(8,128)(2,1)} %param.9, bf16[1,512,3328]{2,1,0:T(8,128)(2,1)} %all-gather.10.cloned.1.call-done, bf16[1,512,3328]{2,1,0:T(8,128)(2,1)} %all-gather.8.cloned.1.call-done), kind=kOutput, calls=%fused_computation.19 | convolution fusion | flops 3503816704 | bytes 14680064 | tf_op jit(solution)/shard_map/dot_general | solution.py:49
  229.5 56.7 %reduce-scatter.5.cloned.1.call-done = f32[32,3328]{1,0:T(8,128)} async-done(((f32[512,3328]{1,0:T(8,128)}), f32[32,3328]{1,0:T(8,128)}) %reduce-scatter.5.cloned.1.call-update) | async-done | bytes 426000 | tf_op jit(solution)/shard_map/reduce_scatter | solution.py:30
  286.1 0.0 copy-done.3
  286.1 0.0 copy-done.4
  286.1 1.9 fusion.31
  288.0 2.7 copy.23
  290.7 0.0 copy-start.1
  290.7 1.6 copy.24
  292.3 92.9 %all-gather.6.cloned.1.call-done = bf16[1024,3328]{0,1:T(8,128)(2,1)} async-done(((bf16[128,3328]{0,1:T(8,128)(2,1)}), bf16[1024,3328]{0,1:T(8,128)(2,1)}) %all-gather.6.cloned.1.call-update) | async-done | bytes 6815760 | tf_op jit(solution)/shard_map/all_gather | solution.py:61
  385.2 9.9 %copy.22 = bf16[1024,3328]{1,0:T(8,128)(2,1)} copy(bf16[1024,3328]{0,1:T(8,128)(2,1)} %all-gather.6.cloned.1.call-done) | data formatting | bytes 13631488
  395.1 0.0 copy-done.1
Async XLA Ops:
  7.2 79.5 %copy-start = (bf16[1,512,1024]{2,1,0:T(8,128)(2,1)S(1)}, bf16[1,512,1024]{2,1,0:T(8,128)(2,1)}, u32[]{:S(2)}) copy-start(bf16[1,512,1024]{2,1,0:T(8,128)(2,1)} %param.6) | copy-start | bytes 3145732
  7.2 41.4 %all-gather.10.cloned.1.call-start = ((), (), s32[]{:S(2)}) async-start(), calls=%async_computation.5 | async-start | bytes 3620864 | tf_op jit(solution)/shard_map/all_gather | solution.py:43
  7.9 78.7 %all-gather.8.cloned.1.call-start = ((), (), s32[]{:S(2)}) async-start(), calls=%async_computation.4 | async-start | bytes 3620864 | tf_op jit(solution)/shard_map/all_gather | solution.py:44
  8.7 204.9 %reduce-scatter.7.cloned.1.call-start = ((), (), s32[]{:S(2)}) async-start(), calls=%async_computation.6 | async-start | bytes 7667712
  109.7 176.5 %reduce-scatter.5.cloned.1.call-start = ((), (), s32[]{:S(2)}) async-start(), calls=%async_computation.2 | async-start | bytes 7241728 | tf_op jit(solution)/shard_map/reduce_scatter | solution.py:30
  118.3 1.9 copy-start.2
  118.3 266.9 %all-gather.6.cloned.1.call-start = ((), (), s32[]{:S(2)}) async-start(), calls=%async_computation.3 | async-start | bytes 7667712 | tf_op jit(solution)/shard_map/all_gather | solution.py:61
  219.1 67.0 %copy-start.3 = (bf16[1,32,3328]{2,1,0:T(8,128)(2,1)S(1)}, bf16[1,32,3328]{2,1,0:T(8,128)(2,1)}, u32[]{:S(2)}) copy-start(bf16[1,32,3328]{2,1,0:T(8,128)(2,1)} %param.7) | copy-start | bytes 638980
  219.2 67.0 %copy-start.4 = (bf16[1,32,3328]{2,1,0:T(8,128)(2,1)S(1)}, bf16[1,32,3328]{2,1,0:T(8,128)(2,1)}, u32[]{:S(2)}) copy-start(bf16[1,32,3328]{2,1,0:T(8,128)(2,1)} %param.8) | copy-start | bytes 638980
  290.7 104.4 %copy-start.1 = (bf16[1,512,1024]{2,1,0:T(8,128)(2,1)S(1)}, bf16[1,512,1024]{2,1,0:T(8,128)(2,1)}, u32[]{:S(2)}) copy-start(bf16[1,512,1024]{2,1,0:T(8,128)(2,1)} %param.6) | copy-start | bytes 3145732
Sparse Core Ops, SparseCore 0:
  9.7 38.7 all-gather.9
  50.2 36.3 all-gather.7
  109.8 103.7 reduce-scatter.6
  216.4 69.6 reduce-scatter.4
  288.2 96.9 all-gather.5
where the time goes:
time: 403 us; the launch traced here: 402 us
  waiting for transfers between devices  308 us (76%)
  local copies, waits for them, and re-layouts  41.6 us (10%)
  matrix products  32 us (8%)
  between operations  13.8 us (3%)
  other arithmetic  5.88 us (1%)
    all_gather x1, waiting for transfers between devices, local(): lax.all_gather(updated.astype(jnp.bfloat16), 'island', axis=0, tiled=True)  92.9 us
    unnamed x6, waiting for transfers between devices  90.5 us
    reduce_scatter x1, waiting for transfers between devices, local(): lax.psum_scatter(jnp.dot(row_block, weight, preferred_element_type=jnp.fl...  56.7 us
    unnamed x18, local copies, waits for them, and re-layouts  41.6 us
    all_gather x1, waiting for transfers between devices, local(): lax.all_gather(cot_mine, 'section', axis=0, tiled=True)  38.1 us
    all_gather x1, waiting for transfers between devices, local(): lax.all_gather(gate_mine, 'section', axis=0, tiled=True)  29.9 us
    dot_general x1, matrix products, contract_rows(): lax.dot_general(left_rows, right_rows, (((0,), (0,)), ((), ())), preferre...  13.1 us
    dot_general x1, matrix products, local(): lax.dot_general(d_up, weight, (((1,), (1,)), ((), ())), preferred_element...  10.3 us
  transfers between devices with their start and end apart: 5, of which 5 were waited for; matrix products, arithmetic and copies ran while one was open for 11% of the time, Pallas kernels for 0%

commit v1 on v0

--- a/solution.py
+++ b/solution.py
@@ -28,22 +28,17 @@
     weight = weights[0]
     row_block = features
     up_mine = lax.psum_scatter(
-        jnp.dot(row_block, weight, preferred_element_type=jnp.float32),
+        jnp.dot(row_block, weight, preferred_element_type=jnp.float32).astype(jnp.bfloat16),
         "section",
         scatter_dimension=0,
         tiled=True,
-    )
+    ).astype(jnp.float32)
     gate_full = gate_mine.astype(jnp.float32)
     gate_sigma = jax.nn.sigmoid(gate_full)
     gate_grad = (
         cot_mine.astype(jnp.float32) * up_mine * gate_sigma * (1.0 + gate_full * (1.0 - gate_sigma))
     ).astype(jnp.bfloat16)
-    d_up = gated_grad(
-        (
-            lax.all_gather(gate_mine, "section", axis=0, tiled=True),
-            lax.all_gather(cot_mine, "section", axis=0, tiled=True),
-        )
-    )
+    d_up = lax.all_gather(gated_grad((gate_mine, cot_mine)), "section", axis=0, tiled=True)
     row_block = features
     weight_grad = contract_rows(row_block, d_up)
     pulled_back = lax.dot_general(

time: 403 us -> 364 us (0.903)
  waiting for transfers between devices: 308 us -> 275 us
  matrix products: 32 us -> 25.5 us
    all_gather x2 -> x1, waiting for transfers between devices: 68 us -> 25.5 us  [local(): lax.all_gather(gated_grad((gate_mine, cot_mine)), 'section', axis=0, tile...]
    reduce_scatter x1, waiting for transfers between devices: 56.7 us -> 67.9 us  [local(): lax.psum_scatter(jnp.dot(row_block, weight, preferred_element_type=jnp.fl...]
    all_gather x1, waiting for transfers between devices: 92.9 us -> 83.7 us  [local(): lax.all_gather(updated.astype(jnp.bfloat16), 'island', axis=0, tiled=True)]
    unnamed x6 -> x5, waiting for transfers between devices: 90.5 us -> 98.3 us
    dot_general x1, matrix products: 13.1 us -> 8.86 us  [contract_rows(): lax.dot_general(left_rows, right_rows, (((0,), (0,)), ((), ())), preferre...]
  transfers between devices with their start and end apart: 5 -> 4, of which waited for: 5 -> 4; matrix products, arithmetic and copies ran while one was open for 11% -> 8% of each run, Pallas kernels for 0% -> 0%
where the time goes in v1:
time: 364 us; the launch traced here: 363 us
  waiting for transfers between devices  275 us (76%)
  local copies, waits for them, and re-layouts  42.3 us (12%)
  matrix products  25.5 us (7%)
  between operations  13.8 us (4%)
  other arithmetic  5.9 us (2%)
    unnamed x5, waiting for transfers between devices  98.3 us
    all_gather x1, waiting for transfers between devices, local(): lax.all_gather(updated.astype(jnp.bfloat16), 'island', axis=0, tiled=True)  83.7 us
    reduce_scatter x1, waiting for transfers between devices, local(): lax.psum_scatter(jnp.dot(row_block, weight, preferred_element_type=jnp.fl...  67.9 us
    unnamed x18, local copies, waits for them, and re-layouts  42.3 us
    all_gather x1, waiting for transfers between devices, local(): lax.all_gather(gated_grad((gate_mine, cot_mine)), 'section', axis=0, tile...  25.5 us
    dot_general x1, matrix products, contract_rows(): lax.dot_general(left_rows, right_rows, (((0,), (0,)), ((), ())), preferre...  8.86 us
    dot_general x1, matrix products, local(): lax.dot_general(d_up, weight, (((1,), (1,)), ((), ())), preferred_element...  8.65 us
    dot_general x1, matrix products, local(): jnp.dot(row_block, weight, preferred_element_type=jnp.float32)  7.98 us
  transfers between devices with their start and end apart: 4, of which 4 were waited for; matrix products, arithmetic and copies ran while one was open for 8% of the time, Pallas kernels for 0%

profile of v1, /device:TPU:0, one launch (start us, length us, event | category | flops | bytes accessed | tf_op | source)
XLA Modules:
  0.0 363.0 jit_solution(5528276983916943320)
XLA Ops:
  7.2 0.0 copy-start
  7.2 0.0 reduce-scatter.5.cloned.1.call-start
  7.2 1.2 copy-done
  8.4 8.0 %fusion.5 = bf16[512,3328]{1,0:T(8,128)(2,1)} fusion(bf16[1,1024,3328]{2,1,0:T(8,128)(2,1)} %param.9, bf16[1,512,1024]{2,1,0:T(8,128)(2,1)S(1)} %copy-done), kind=kOutput, calls=%fused_computation.6 | convolution fusion | flops 3491364864 | bytes 11272192 | tf_op jit(solution)/shard_map/dot_general | solution.py:31
  16.4 0.0 copy-start.3
  16.4 0.0 copy-start.4
  16.4 0.0 reduce-scatter.5.cloned.1.call-update
  16.4 0.0 all-gather.3.cloned.1.call-start
  16.5 67.9 %reduce-scatter.5.cloned.1.call-done = bf16[32,3328]{1,0:T(8,128)(2,1)} async-done(((bf16[512,3328]{1,0:T(8,128)(2,1)}), bf16[32,3328]{1,0:T(8,128)(2,1)}) %reduce-scatter.5.cloned.1.call-update) | async-done | bytes 213008 | tf_op jit(solution)/shard_map/reduce_scatter | solution.py:30
  84.4 0.0 copy-done.3
  84.4 0.0 copy-done.4
  84.4 1.9 fusion.25
  86.3 0.0 all-gather.3.cloned.1.call-update
  86.3 0.0 reduce-scatter.7.cloned.1.call-start
  86.4 10.0 %copy.18 = bf16[1,1024,3328]{1,2,0:T(8,128)(2,1)} copy(bf16[1,1024,3328]{2,1,0:T(8,128)(2,1)} %param.9) | data formatting | bytes 13631488 | tf_op args[3]
  96.3 25.5 %all-gather.3.cloned.1.call-done = bf16[512,3328]{1,0:T(8,128)(2,1)} async-done(((bf16[32,3328]{1,0:T(8,128)(2,1)}), bf16[512,3328]{1,0:T(8,128)(2,1)}) %all-gather.3.cloned.1.call-update) | async-done | bytes 3407888 | tf_op jit(solution)/shard_map/all_gather | solution.py:41
  121.8 8.9 %fusion = bf16[1024,3328]{0,1:T(8,128)(2,1)} fusion(bf16[512,3328]{1,0:T(8,128)(2,1)} %all-gather.3.cloned.1.call-done, bf16[1,1024,3328]{1,2,0:T(8,128)(2,1)} %copy.18, bf16[1,512,1024]{2,1,0:T(8,128)(2,1)S(1)} %copy-done), kind=kOutput, calls=%fused_computation.1 | convolution fusion | flops 3503292416 | bytes 18087936 | tf_op jit(solution)/shard_map/dot_general | solution.py:12
  130.7 9.6 %copy.25 = bf16[1024,3328]{1,0:T(8,128)(2,1)} copy(bf16[1024,3328]{0,1:T(8,128)(2,1)} %fusion) | data formatting | bytes 13631488
  140.2 0.0 copy-start.2
  140.3 0.0 reduce-scatter.7.cloned.1.call-update
  140.3 0.0 all-gather.5.cloned.1.call-start
  140.3 1.4 copy-done.2
  141.7 1.6 copy.21
  143.3 2.7 copy.20
  146.0 98.2 %reduce-scatter.7.cloned.1.call-done = bf16[128,3328]{1,0:T(8,128)(2,1)} async-done(((bf16[1024,3328]{1,0:T(8,128)(2,1)}), bf16[128,3328]{1,0:T(8,128)(2,1)}) %reduce-scatter.7.cloned.1.call-update) | async-done | bytes 851984
  244.2 1.5 copy.26
  245.8 4.0 %fusion.26 = (bf16[128,3328]{0,1:T(8,128)(2,1)}, f32[128,3328]{0,1:T(8,128)}, f32[128,3328]{0,1:T(8,128)S(1)}) fusion(f32[128,3328]{0,1:T(8,128)} %copy.21, f32[128,3328]{0,1:T(8,128)} %copy.20, bf16[128,3328]{0,1:T(8,128)(2,1)S(1)} %copy.26), kind=kLoop, calls=%fused_computation.28 | loop fusion | flops 4259840 | bytes 8519680 | tf_op jit(solution)/shard_map/convert_element_type | solution.py:56
  249.8 0.0 all-gather.5.cloned.1.call-update
  249.8 8.7 %fusion.11 = bf16[1,512,1024]{2,1,0:T(8,128)(2,1)} fusion(bf16[512,3328]{1,0:T(8,128)(2,1)} %all-gather.3.cloned.1.call-done, bf16[1,1024,3328]{2,1,0:T(8,128)(2,1)} %param.9), kind=kOutput, calls=%fused_computation.11 | convolution fusion | flops 3490185216 | bytes 11272192 | tf_op jit(solution)/shard_map/dot_general | solution.py:44
  258.4 2.7 copy.23
  261.2 1.6 copy.24
  262.8 83.7 %all-gather.5.cloned.1.call-done = bf16[1024,3328]{0,1:T(8,128)(2,1)} async-done(((bf16[128,3328]{0,1:T(8,128)(2,1)}), bf16[1024,3328]{0,1:T(8,128)(2,1)}) %all-gather.5.cloned.1.call-update) | async-done | bytes 6815760 | tf_op jit(solution)/shard_map/all_gather | solution.py:56
  346.5 0.0 copy-start.1
  346.5 10.0 %copy.22 = bf16[1024,3328]{1,0:T(8,128)(2,1)} copy(bf16[1024,3328]{0,1:T(8,128)(2,1)} %all-gather.5.cloned.1.call-done) | data formatting | bytes 13631488
  356.5 0.0 copy-done.1
Async XLA Ops:
  7.2 1.2 copy-start
  7.2 77.2 %reduce-scatter.5.cloned.1.call-start = ((), (), s32[]{:S(2)}) async-start(), calls=%async_computation.3 | async-start | bytes 3620864 | tf_op jit(solution)/shard_map/reduce_scatter | solution.py:30
  16.4 68.0 %copy-start.3 = (bf16[1,32,3328]{2,1,0:T(8,128)(2,1)S(1)}, bf16[1,32,3328]{2,1,0:T(8,128)(2,1)}, u32[]{:S(2)}) copy-start(bf16[1,32,3328]{2,1,0:T(8,128)(2,1)} %param.7) | copy-start | bytes 638980
  16.4 68.0 %copy-start.4 = (bf16[1,32,3328]{2,1,0:T(8,128)(2,1)S(1)}, bf16[1,32,3328]{2,1,0:T(8,128)(2,1)}, u32[]{:S(2)}) copy-start(bf16[1,32,3328]{2,1,0:T(8,128)(2,1)} %param.8) | copy-start | bytes 638980
  16.4 105.4 %all-gather.3.cloned.1.call-start = ((), (), s32[]{:S(2)}) async-start(), calls=%async_computation.2 | async-start | bytes 3620864 | tf_op jit(solution)/shard_map/all_gather | solution.py:41
  86.3 157.9 %reduce-scatter.7.cloned.1.call-start = ((), (), s32[]{:S(2)}) async-start(), calls=%async_computation.5 | async-start | bytes 7667712
  140.2 1.5 copy-start.2
  140.3 206.2 %all-gather.5.cloned.1.call-start = ((), (), s32[]{:S(2)}) async-start(), calls=%async_computation.4 | async-start | bytes 7667712 | tf_op jit(solution)/shard_map/all_gather | solution.py:56
  346.5 10.0 %copy-start.1 = (bf16[1,512,1024]{2,1,0:T(8,128)(2,1)S(1)}, bf16[1,512,1024]{2,1,0:T(8,128)(2,1)}, u32[]{:S(2)}) copy-start(bf16[1,512,1024]{2,1,0:T(8,128)(2,1)} %param.6) | copy-start | bytes 3145732
Sparse Core Ops, SparseCore 0:
  16.5 67.8 reduce-scatter.4
  86.8 35.0 all-gather.2
  140.4 103.8 reduce-scatter.6
  249.9 96.5 all-gather.4

commit v2 on v1

v2 whole, which is shorter than its diff:
```python
import functools

import jax
import jax.numpy as jnp
from jax import lax
from jax.experimental import pallas as pl
from jax.experimental.pallas import tpu as pltpu
from jax.sharding import PartitionSpec as P

inner_rate = 0.0005
outer_rate = 0.7
nesterov_mu = 0.9

MESH = pl.DeviceIdType.MESH
F32 = jnp.float32
BF16 = jnp.bfloat16

W = 256
N_Z = 4
N_ISL = 8
PLANE = 8
TB = 32
RB = 128
LAG = 6


def kernel(
    n_chunk,
    x_hbm, gate_hbm, cot_hbm, w_hbm, outer_hbm, mom_hbm,
    ig_out, gg_out, nw_out, no_out, nm_out,
    x_v, xt_v, gate_v, cot_v, outer_v, mom_v, w_v, dup_v,
    inner_v, r1_v, r2_v, xs_v, rx_v,
    ups_v, upr_v, upo_v, upt_v, upp_v, acc_v,
    in_sem, w_sem, snd, r_dup, r_sib, r_s1, r_raw, r_acc, r_x,
    r_gx, r_go, r_gp, r_gf, r_ups, r_upp,
):
    sec = lax.axis_index("section")
    isl = lax.axis_index("island")
    core = lax.rem(sec, 2)
    place = sec // 2
    z = lax.rem(isl, N_Z)
    xh = isl // N_Z
    up_z = lax.rem(z + 1, N_Z)
    dn_z = lax.rem(z + N_Z - 1, N_Z)
    op_z = lax.rem(z + 2, N_Z)
    to_up = (sec, xh * N_Z + up_z)
    to_dn = (sec, xh * N_Z + dn_z)
    to_x = (sec, (1 - xh) * N_Z + z)
    to_sib = (place * 2 + 1 - core, isl)

    def peer(k):
        return (lax.rem(place + k, PLANE) * 2 + core, isl)

    def remote(src, dst, c, recv, device):
        return pltpu.make_async_remote_copy(
            src_ref=src, dst_ref=dst, send_sem=snd.at[c], recv_sem=recv,
            device_id=device, device_id_type=MESH,
        )

    def arrived(dst, recv):
        pltpu.make_async_copy(dst, dst, recv).wait()

    def cols(c):
        return pl.ds(pl.multiple_of(c * W, W), W)

    barrier = pltpu.get_barrier_semaphore()
    for device in (to_up, to_dn, to_x, to_sib):
        pl.semaphore_signal(barrier, inc=1, device_id=device, device_id_type=MESH)
    for k in range(1, PLANE):
        pl.semaphore_signal(barrier, inc=1, device_id=peer(k), device_id_type=MESH)

    def w_copy(c):
        return pltpu.make_async_copy(w_hbm.at[:, :, cols(c)], w_v.at[c], w_sem.at[c])

    in_copies = [
        pltpu.make_async_copy(gate_hbm, gate_v, in_sem.at[0]),
        pltpu.make_async_copy(cot_hbm, cot_v, in_sem.at[1]),
        pltpu.make_async_copy(x_hbm.at[:, 0], x_v.at[0], in_sem.at[2]),
        pltpu.make_async_copy(x_hbm.at[:, 1], x_v.at[1], in_sem.at[3]),
        pltpu.make_async_copy(outer_hbm, outer_v, in_sem.at[4]),
        pltpu.make_async_copy(mom_hbm, mom_v, in_sem.at[5]),
    ]
    for copy in in_copies[:4]:
        copy.start()

    def dup_form(c):
        g = gate_v[:, cols(c)].astype(F32)
        s = jax.nn.sigmoid(g)
        d = cot_v[:, cols(c)].astype(F32) * g * s
        dup_v[c * 16 + core * PLANE + place] = d.astype(BF16)

    def dup_send(c):
        mine = dup_v.at[c * 16 + core * PLANE + place]
        for k in range(1, PLANE):
            remote(mine, mine, c, r_dup.at[c], peer(k)).start()

    def dup_share(c):
        arrived(dup_v.at[pl.ds(c * 16 + core * PLANE, PLANE - 1)], r_dup.at[c])
        half = dup_v.at[pl.ds(c * 16 + core * PLANE, PLANE)]
        remote(half, half, c, r_sib.at[c], to_sib).start()

    def inner_form(c):
        arrived(dup_v.at[pl.ds(c * 16 + (1 - core) * PLANE, PLANE)], r_sib.at[c])
        d_up = dup_v[pl.ds(c * 16, 16)].reshape(16 * TB, W)
        for half in range(2):
            lhs = xt_v[half].reshape(N_Z * RB, 16 * TB)
            grad = jnp.dot(lhs, d_up, preferred_element_type=F32)
            for rel in range(N_Z):
                block = half * N_Z + lax.rem(z + rel, N_Z)
                w_part = w_v[c, block].astype(F32)
                inner_v[c, half, rel] = (
                    w_part - inner_rate * grad[rel * RB : (rel + 1) * RB]
                ).astype(BF16)
        remote(inner_v.at[c, 0, 2], r1_v.at[c, 0], c, r_s1.at[c, 0], to_up).start()
        remote(inner_v.at[c, 1, 2], r1_v.at[c, 1], c, r_s1.at[c, 1], to_dn).start()
        remote(inner_v.at[c, 1, 1], r2_v.at[c, 0, 1], c, r_raw.at[c, 0], to_up).start()
        remote(inner_v.at[c, 0, 3], r2_v.at[c, 1, 0], c, r_raw.at[c, 1], to_dn).start()

    def rs_second(c):
        arrived(r1_v.at[c, 0], r_s1.at[c, 0])
        inner_v[c, 0, 1] = (inner_v[c, 0, 1].astype(F32) + r1_v[c, 0].astype(F32)).astype(BF16)
        remote(inner_v.at[c, 0, 1], r2_v.at[c, 0, 0], c, r_acc.at[c, 0], to_up).start()
        arrived(r1_v.at[c, 1], r_s1.at[c, 1])
        inner_v[c, 1, 3] = (inner_v[c, 1, 3].astype(F32) + r1_v[c, 1].astype(F32)).astype(BF16)
        remote(inner_v.at[c, 1, 3], r2_v.at[c, 1, 1], c, r_acc.at[c, 1], to_dn).start()

    def rs_x(c):
        arrived(r2_v.at[c, 0, 1], r_raw.at[c, 0])
        arrived(r2_v.at[c, 1, 0], r_raw.at[c, 1])
        arrived(r2_v.at[c, 0, 0], r_acc.at[c, 0])
        arrived(r2_v.at[c, 1, 1], r_acc.at[c, 1])
        xs_v[c] = (
            inner_v[c, 1 - xh, 0].astype(F32)
            + r2_v[c, 0, 1 - xh].astype(F32)
            + r2_v[c, 1, 1 - xh].astype(F32)
        ).astype(BF16)
        remote(xs_v.at[c], rx_v.at[c], c, r_x.at[c], to_x).start()

    def block_of(c, half, zz):
        return nw_out.at[half * N_Z + zz, :, cols(c)]

    def update(c):
        arrived(rx_v.at[c], r_x.at[c])
        total = (
            inner_v[c, xh, 0].astype(F32)
            + r2_v[c, 0, xh].astype(F32)
            + r2_v[c, 1, xh].astype(F32)
            + rx_v[c].astype(F32)
        )
        own = outer_v[:, cols(c)]
        delta = own - total * (1.0 / N_ISL)
        moment = nesterov_mu * mom_v[:, cols(c)] + delta
        new = own - outer_rate * (delta + nesterov_mu * moment)
        nm_out[:, cols(c)] = moment
        no_out[:, cols(c)] = new
        nw_out[isl, :, cols(c)] = new.astype(BF16)
        mine = block_of(c, xh, z)
        remote(mine, mine, c, r_gx.at[c], to_x).start()
        remote(mine, mine, c, r_go.at[c, 0], to_up).start()
        remote(mine, mine, c, r_go.at[c, 1], to_dn).start()

    def ag_partner(c):
        theirs = block_of(c, 1 - xh, z)
        arrived(theirs, r_gx.at[c])
        remote(theirs, theirs, c, r_gp.at[c, 0], to_up).start()
        remote(theirs, theirs, c, r_gp.at[c, 1], to_dn).start()

    def ag_forward(c):
        arrived(block_of(c, xh, dn_z), r_go.at[c, 0])
        arrived(block_of(c, 1 - xh, dn_z), r_gp.at[c, 0])
        low = block_of(c, 0, dn_z)
        remote(low, low, c, r_gf.at[c, 0], to_up).start()
        arrived(block_of(c, xh, up_z), r_go.at[c, 1])
        arrived(block_of(c, 1 - xh, up_z), r_gp.at[c, 1])
        high = block_of(c, 1, up_z)
        remote(high, high, c, r_gf.at[c, 1], to_dn).start()

    def ag_last(c):
        arrived(block_of(c, 0, op_z), r_gf.at[c, 0])
        arrived(block_of(c, 1, op_z), r_gf.at[c, 1])

    def up_form(c):
        w_all = w_v[c].reshape(N_ISL * RB, W)
        lhs = x_v[1 - core].reshape(PLANE * TB, N_ISL * RB)
        ups_v[c] = jnp.dot(lhs, w_all, preferred_element_type=F32).astype(BF16)
        remote(ups_v.at[c], upr_v.at[c], c, r_ups.at[c], to_sib).start()
        lhs = x_v[core].reshape(PLANE * TB, N_ISL * RB)
        upo_v[c] = jnp.dot(lhs, w_all, preferred_element_type=F32).astype(BF16)

    def up_add(c):
        arrived(upr_v.at[c], r_ups.at[c])
        both = upo_v[c].astype(F32) + upr_v[c].astype(F32)
        upt_v[pl.ds(c * PLANE, PLANE)] = both.astype(BF16).reshape(PLANE, TB, W)
        for k in range(1, PLANE):
            to = lax.rem(place + k, PLANE)
            remote(
                upt_v.at[c * PLANE + to], upp_v.at[c * PLANE + place], c, r_upp.at[c], peer(k)
            ).start()

    def up_last(c):
        arrived(upp_v.at[pl.ds(c * PLANE, PLANE - 1)], r_upp.at[c])
        up = upt_v[c * PLANE + place].astype(F32)
        for k in range(1, PLANE):
            up = up + upp_v[c * PLANE + lax.rem(place + k, PLANE)].astype(F32)
        g = gate_v[:, cols(c)].astype(F32)
        s = jax.nn.sigmoid(g)
        out = cot_v[:, cols(c)].astype(F32) * up * s * (1.0 + g * (1.0 - s))
        gg_out[:, cols(c)] = out.astype(BF16)

    def ig_form(c):
        d_up = dup_v[pl.ds(c * 16, 16)].reshape(16 * TB, W)
        w_all = w_v[c].reshape(N_ISL * RB, W)
        part = lax.dot_general(
            d_up, w_all, (((1,), (1,)), ((), ())), preferred_element_type=F32
        )
        acc_v[...] += part

    in_copies[0].wait()
    in_copies[1].wait()
    w_copy(0).start()
    dup_form(0)
    pl.semaphore_wait(barrier, 3 + PLANE)
    dup_send(0)

    @pl.loop(1, 3)
    def _(c):
        dup_form(c)
        dup_send(c)

    @pl.loop(1, n_chunk)
    def _(c):
        w_copy(c).start()

    in_copies[4].start()
    in_copies[5].start()
    in_copies[2].wait()
    in_copies[3].wait()
    for block in range(N_ISL):
        piece = x_v[:, :, :, block * RB : (block + 1) * RB].reshape(16 * TB, RB)
        rel = lax.rem(block % N_Z + N_Z - z, N_Z)
        xt_v[block // N_Z, rel] = piece.T
    acc_v[...] = jnp.zeros_like(acc_v)
    dup_share(0)

    def at(c, lo, hi, *steps):
        @pl.when((c >= lo) & (c < hi))
        def _():
            for step in steps:
                step(c)

    @pl.loop(0, n_chunk + LAG)
    def _(t):
        def first(c):
            dup_form(c)
            dup_send(c)

        at(t + 3, 0, n_chunk, first)
        at(t + 1, 0, n_chunk, dup_share)

        def second(c):
            w_copy(c).wait()
            inner_form(c)
            up_form(c)

        at(t, 0, n_chunk, second)
        at(t - 1, 0, n_chunk, rs_second)
        at(t - 2, 0, n_chunk, rs_x)

        @pl.when(t == 3)
        def _():
            in_copies[4].wait()
            in_copies[5].wait()

        at(t - 3, 0, n_chunk, update)
        at(t - 4, 0, n_chunk, ag_partner)
        at(t - 5, 0, n_chunk, ag_forward)
        at(t, 0, n_chunk, ig_form)
        at(t - 2, 0, n_chunk, up_add)
        at(t - 5, 0, n_chunk, up_last)
        at(t - 6, 0, n_chunk, ag_last)

    for half in range(2):
        ig_out[:, half] = acc_v[half * PLANE * TB : (half + 1) * PLANE * TB].astype(BF16).reshape(
            PLANE, TB, N_ISL * RB
        )

    sent = (2 * 7 * TB + 2 * PLANE * TB + 6 * RB + RB + 3 * RB + 2 * RB + 2 * RB) // TB

    @pl.loop(0, n_chunk)
    def _(c):
        arrived(dup_v.at[pl.ds(0, sent)], snd.at[c])


def local(inputs, gate_pre, up_cot, weights, outer, momentum):
    d_loc, fs = weights.shape[1], weights.shape[2]
    tok = inputs.shape[1]
    c = fs // W
    dma = pltpu.SemaphoreType.DMA
    vmem = pl.BlockSpec(memory_space=pltpu.VMEM)
    hbm = pl.BlockSpec(memory_space=pltpu.HBM)
    ig, gg, nw, no, nm = pl.pallas_call(
        functools.partial(kernel, c),
        out_shape=(
            jax.ShapeDtypeStruct((PLANE, 2, TB, d_loc), BF16),
            jax.ShapeDtypeStruct((TB, fs), BF16),
            jax.ShapeDtypeStruct((N_ISL, RB, fs), BF16),
            jax.ShapeDtypeStruct((RB, fs), F32),
            jax.ShapeDtypeStruct((RB, fs), F32),
        ),
        in_specs=[hbm] * 6,
        out_specs=(vmem,) * 5,
        scratch_shapes=[
            pltpu.VMEM((2, PLANE, TB, d_loc), BF16),
            pltpu.VMEM((2, N_Z, RB, tok), BF16),
            pltpu.VMEM((TB, fs), BF16),
            pltpu.VMEM((TB, fs), BF16),
            pltpu.VMEM((RB, fs), F32),
            pltpu.VMEM((RB, fs), F32),
            pltpu.VMEM((c, N_ISL, RB, W), BF16),
            pltpu.VMEM((c * 16, TB, W), BF16),
            pltpu.VMEM((c, 2, N_Z, RB, W), BF16),
            pltpu.VMEM((c, 2, RB, W), BF16),
            pltpu.VMEM((c, 2, 2, RB, W), BF16),
            pltpu.VMEM((c, RB, W), BF16),
            pltpu.VMEM((c, RB, W), BF16),
            pltpu.VMEM((c, PLANE * TB, W), BF16),
            pltpu.VMEM((c, PLANE * TB, W), BF16),
            pltpu.VMEM((c, PLANE * TB, W), BF16),
            pltpu.VMEM((c * PLANE, TB, W), BF16),
            pltpu.VMEM((c * PLANE, TB, W), BF16),
            pltpu.VMEM((tok, d_loc), F32),
            dma((6,)),
            dma((c,)),
            dma((c,)),
            dma((c,)),
            dma((c,)),
            dma((c, 2)),
            dma((c, 2)),
            dma((c, 2)),
            dma((c,)),
            dma((c,)),
            dma((c, 2)),
            dma((c, 2)),
            dma((c, 2)),
            dma((c,)),
            dma((c,)),
        ],
        compiler_params=pltpu.CompilerParams(
            collective_id=0, has_side_effects=True, vmem_limit_bytes=48 * 2**20
        ),
        cost_estimate=pl.CostEstimate(
            flops=6 * tok * d_loc * fs, bytes_accessed=8 * d_loc * fs, transcendentals=0
        ),
    )(
        inputs.reshape(PLANE, 2, TB, d_loc),
        gate_pre[0],
        up_cot[0],
        weights.reshape(N_ISL, RB, fs),
        outer,
        momentum,
    )
    return (
        ig.reshape(1, tok, d_loc),
        gg[None],
        nw.reshape(d_loc, fs),
        no,
        nm,
    )


def solution(mesh):
    placed = (
        P("island", None, "section"),
        P("island", "section", None),
        P("island", "section", None),
        P("island", "section", None),
        P(("section", "island"), None),
        P(("section", "island"), None),
    )
    return jax.shard_map(
        local,
        mesh=mesh,
        in_specs=placed,
        out_specs=(
            P("island", None, "section"),
            P("island", "section", None),
            P("section", None),
            P(("section", "island"), None),
            P(("section", "island"), None),
        ),
        check_vma=False,
    )
```

time: 364 us -> 146 us (0.40)
  waiting for transfers between devices: 275 us -> 0 us
  Pallas kernels: 0 us -> 132 us
  local copies, waits for them, and re-layouts: 42.3 us -> 13.4 us
  matrix products: 25.5 us -> 0 us
  between operations: 13.8 us -> 0.65 us
  other arithmetic: 5.9 us -> 0 us
    pallas_call x0 -> x1, Pallas kernels: none -> 132 us  [local(): pl.pallas_call(functools.partial(kernel, c), out_shape=(jax.ShapeDtypeStr...]
    all_gather x2 -> x0, waiting for transfers between devices: 109 us -> none  [the longest x1 83.7 us: local(): lax.all_gather(updated.astype(jnp.bfloat16), 'island', axis=0, tiled=True)]
    unnamed x5 -> x0, waiting for transfers between devices: 98.3 us -> none
    reduce_scatter x1 -> x0, waiting for transfers between devices: 67.9 us -> none  [local(): lax.psum_scatter(jnp.dot(row_block, weight, preferred_element_type=jnp.fl...]
    unnamed x18 -> x11, local copies, waits for them, and re-layouts: 42.3 us -> 13.4 us
    dot_general x3 -> x0, matrix products: 25.5 us -> none  [the longest x1 8.86 us: contract_rows(): lax.dot_general(left_rows, right_rows, (((0,), (0,)), ((), ())), preferre...]
    convert_element_type x1 -> x0, other arithmetic: 3.99 us -> none  [local(): updated.astype(jnp.bfloat16)]
  transfers between devices with their start and end apart: 4 -> 0, of which waited for: 4 -> 0; matrix products, arithmetic and copies ran while one was open for 8% -> 0% of each run, Pallas kernels for 0% -> 0%
where the time goes in v2:
time: 146 us
  Pallas kernels  132 us (90%)
  local copies, waits for them, and re-layouts  13.4 us (9%)
    pallas_call x1, Pallas kernels, local(): pl.pallas_call(functools.partial(kernel, c), out_shape=(jax.ShapeDtypeStr...  132 us
    unnamed x11, local copies, waits for them, and re-layouts  13.4 us

profile of v2, /device:TPU:0, one launch (start us, length us, event | category | flops | bytes accessed | tf_op | source)
XLA Modules:
  0.0 145.8 jit_solution(15561069430762906408)
XLA Ops:
  0.6 0.0 copy-start
  0.6 1.2 copy-done
  1.9 0.0 copy-start.1
  1.9 0.9 copy-done.1
  2.8 0.0 copy-start.2
  2.8 0.9 copy-done.2
  3.7 131.8 %shard_map.101 = (bf16[8,2,32,1024]{3,2,1,0:T(8,128)(2,1)S(1)}, bf16[32,3328]{1,0:T(8,128)(2,1)S(1)}, bf16[8,128,3328]{2,1,0:T(8,128)(2,1)}, f32[128,3328]{1,0:T(8,128)S(1)}, f32[128,3328]{1,0:T(8,128)S(1)}) custom-call(bf16[8,2,32,1024]{3,2,1,0:T(8,128)(2,1)S(1)} %bitcast.9, bf16[32,3328]{1,0:T(8,128)(2,1)S(1)} %bitcast.10, bf16[32,3328]{1,0:T(8,128)(2,1)S(1)} %bitcast.11, ...), custom_call_target="tpu_custom_call" | custom-call | flops 10468982784 | bytes 27262976 | tf_op jit(solution)/shard_map/pallas_call | solution.py:301
  135.5 1.0 copy.16
  136.5 0.7 copy.17
  137.1 6.2 %copy.18 = bf16[1024,3328]{1,0:T(8,128)(2,1)} copy(bf16[1024,3328]{1,0:T(8,128)(2,1)} %bitcast.12) | data formatting | bytes 13631488
  143.4 1.2 copy.19
  144.6 1.2 copy.20
Async XLA Ops:
  0.6 1.2 copy-start
  1.9 0.9 copy-start.1
  2.8 0.9 copy-start.2

commit v3 on v2

--- a/solution.py
+++ b/solution.py
@@ -21,7 +21,10 @@
 PLANE = 8
 TB = 32
 RB = 128
-LAG = 6
+HB = RB // 2
+X_EVERY, X_AT = 4, 1
+LAG_A, LAG_B, LAG_C, LAG_D, LAG_E, LAG_F = 1, 2, 3, 4, 5, 6
+LAG_UA, LAG_UB = 2, 5
 
 
 def kernel(
@@ -29,10 +32,10 @@
     x_hbm, gate_hbm, cot_hbm, w_hbm, outer_hbm, mom_hbm,
     ig_out, gg_out, nw_out, no_out, nm_out,
     x_v, xt_v, gate_v, cot_v, outer_v, mom_v, w_v, dup_v,
-    inner_v, r1_v, r2_v, xs_v, rx_v,
+    inner_v, r1_v, r2_v, xs_v, rx_v, rxx_v,
     ups_v, upr_v, upo_v, upt_v, upp_v, acc_v,
     in_sem, w_sem, snd, r_dup, r_sib, r_s1, r_raw, r_acc, r_x,
-    r_gx, r_go, r_gp, r_gf, r_ups, r_upp,
+    r_gx, r_go, r_gp, r_gf, r_gz, r_ups, r_upp,
 ):
     sec = lax.axis_index("section")
     isl = lax.axis_index("island")
@@ -102,7 +105,7 @@
     def inner_form(c):
         arrived(dup_v.at[pl.ds(c * 16 + (1 - core) * PLANE, PLANE)], r_sib.at[c])
         d_up = dup_v[pl.ds(c * 16, 16)].reshape(16 * TB, W)
-        for half in range(2):
+        for half in (1 - xh, xh):
             lhs = xt_v[half].reshape(N_Z * RB, 16 * TB)
             grad = jnp.dot(lhs, d_up, preferred_element_type=F32)
             for rel in range(N_Z):
@@ -111,20 +114,25 @@
                 inner_v[c, half, rel] = (
                     w_part - inner_rate * grad[rel * RB : (rel + 1) * RB]
                 ).astype(BF16)
+
+    def add_into(dst, other):
+        dst[...] = (dst[...].astype(F32) + other[...].astype(F32)).astype(BF16)
+
+    def z_first(c):
         remote(inner_v.at[c, 0, 2], r1_v.at[c, 0], c, r_s1.at[c, 0], to_up).start()
         remote(inner_v.at[c, 1, 2], r1_v.at[c, 1], c, r_s1.at[c, 1], to_dn).start()
         remote(inner_v.at[c, 1, 1], r2_v.at[c, 0, 1], c, r_raw.at[c, 0], to_up).start()
         remote(inner_v.at[c, 0, 3], r2_v.at[c, 1, 0], c, r_raw.at[c, 1], to_dn).start()
 
-    def rs_second(c):
+    def z_second(c):
         arrived(r1_v.at[c, 0], r_s1.at[c, 0])
-        inner_v[c, 0, 1] = (inner_v[c, 0, 1].astype(F32) + r1_v[c, 0].astype(F32)).astype(BF16)
+        add_into(inner_v.at[c, 0, 1], r1_v.at[c, 0])
         remote(inner_v.at[c, 0, 1], r2_v.at[c, 0, 0], c, r_acc.at[c, 0], to_up).start()
         arrived(r1_v.at[c, 1], r_s1.at[c, 1])
-        inner_v[c, 1, 3] = (inner_v[c, 1, 3].astype(F32) + r1_v[c, 1].astype(F32)).astype(BF16)
+        add_into(inner_v.at[c, 1, 3], r1_v.at[c, 1])
         remote(inner_v.at[c, 1, 3], r2_v.at[c, 1, 1], c, r_acc.at[c, 1], to_dn).start()
 
-    def rs_x(c):
+    def z_third(c):
         arrived(r2_v.at[c, 0, 1], r_raw.at[c, 0])
         arrived(r2_v.at[c, 1, 0], r_raw.at[c, 1])
         arrived(r2_v.at[c, 0, 0], r_acc.at[c, 0])
@@ -136,17 +144,37 @@
         ).astype(BF16)
         remote(xs_v.at[c], rx_v.at[c], c, r_x.at[c], to_x).start()
 
+    def x_first(c):
+        remote(inner_v.at[c, 1 - xh], rxx_v.at[c // X_EVERY], c, r_x.at[c], to_x).start()
+
+    def x_second(c):
+        got = rxx_v.at[c // X_EVERY]
+        arrived(got, r_x.at[c])
+        low, high = pl.ds(0, HB), pl.ds(HB, HB)
+        far, above, below = (inner_v.at[c, xh, rel] for rel in (2, 1, 3))
+        add_into(far, got.at[2])
+        remote(far.at[low], r1_v.at[c, 0, low], c, r_s1.at[c, 0], to_up).start()
+        remote(far.at[high], r1_v.at[c, 1, low], c, r_s1.at[c, 1], to_dn).start()
+        add_into(above, got.at[1])
+        remote(above.at[high], r2_v.at[c, 0, 0, high], c, r_raw.at[c, 0], to_up).start()
+        add_into(below, got.at[3])
+        remote(below.at[low], r2_v.at[c, 1, 0, low], c, r_raw.at[c, 1], to_dn).start()
+
+    def x_third(c):
+        low, high = pl.ds(0, HB), pl.ds(HB, HB)
+        arrived(r1_v.at[c, 0, low], r_s1.at[c, 0])
+        above = inner_v.at[c, xh, 1, low]
+        add_into(above, r1_v.at[c, 0, low])
+        remote(above, r2_v.at[c, 0, 0, low], c, r_acc.at[c, 0], to_up).start()
+        arrived(r1_v.at[c, 1, low], r_s1.at[c, 1])
+        below = inner_v.at[c, xh, 3, high]
+        add_into(below, r1_v.at[c, 1, low])
+        remote(below, r2_v.at[c, 1, 0, high], c, r_acc.at[c, 1], to_dn).start()
+
     def block_of(c, half, zz):
         return nw_out.at[half * N_Z + zz, :, cols(c)]
 
-    def update(c):
-        arrived(rx_v.at[c], r_x.at[c])
-        total = (
-            inner_v[c, xh, 0].astype(F32)
-            + r2_v[c, 0, xh].astype(F32)
-            + r2_v[c, 1, xh].astype(F32)
-            + rx_v[c].astype(F32)
-        )
+    def update(c, total):
         own = outer_v[:, cols(c)]
         delta = own - total * (1.0 / N_ISL)
         moment = nesterov_mu * mom_v[:, cols(c)] + delta
@@ -159,13 +187,37 @@
         remote(mine, mine, c, r_go.at[c, 0], to_up).start()
         remote(mine, mine, c, r_go.at[c, 1], to_dn).start()
 
-    def ag_partner(c):
+    def z_update(c):
+        arrived(rx_v.at[c], r_x.at[c])
+        update(
+            c,
+            inner_v[c, xh, 0].astype(F32)
+            + r2_v[c, 0, xh].astype(F32)
+            + r2_v[c, 1, xh].astype(F32)
+            + rx_v[c].astype(F32),
+        )
+
+    def x_update(c):
+        half = pl.ds(0, HB)
+        arrived(r2_v.at[c, 0, 0, half], r_raw.at[c, 0])
+        arrived(r2_v.at[c, 1, 0, half], r_raw.at[c, 1])
+        arrived(r2_v.at[c, 0, 0, half], r_acc.at[c, 0])
+        arrived(r2_v.at[c, 1, 0, half], r_acc.at[c, 1])
+        update(
+            c,
+            inner_v[c, xh, 0].astype(F32)
+            + rxx_v[c // X_EVERY, 0].astype(F32)
+            + r2_v[c, 0, 0].astype(F32)
+            + r2_v[c, 1, 0].astype(F32),
+        )
+
+    def z_partner(c):
         theirs = block_of(c, 1 - xh, z)
         arrived(theirs, r_gx.at[c])
         remote(theirs, theirs, c, r_gp.at[c, 0], to_up).start()
         remote(theirs, theirs, c, r_gp.at[c, 1], to_dn).start()
 
-    def ag_forward(c):
+    def z_forward(c):
         arrived(block_of(c, xh, dn_z), r_go.at[c, 0])
         arrived(block_of(c, 1 - xh, dn_z), r_gp.at[c, 0])
         low = block_of(c, 0, dn_z)
@@ -175,9 +227,50 @@
         high = block_of(c, 1, up_z)
         remote(high, high, c, r_gf.at[c, 1], to_dn).start()
 
-    def ag_last(c):
+    def z_last(c):
         arrived(block_of(c, 0, op_z), r_gf.at[c, 0])
         arrived(block_of(c, 1, op_z), r_gf.at[c, 1])
+
+    def half_of(c, half, zz, part):
+        return nw_out.at[half * N_Z + zz, pl.ds(part * HB, HB), cols(c)]
+
+    def x_neighbours(c):
+        below = block_of(c, xh, dn_z)
+        arrived(below, r_go.at[c, 0])
+        part = half_of(c, xh, dn_z, 0)
+        remote(part, part, c, r_gf.at[c, 0], to_up).start()
+        remote(below, below, c, r_gp.at[c, 0], to_x).start()
+        above = block_of(c, xh, up_z)
+        arrived(above, r_go.at[c, 1])
+        part = half_of(c, xh, up_z, 1)
+        remote(part, part, c, r_gf.at[c, 1], to_dn).start()
+        remote(above, above, c, r_gp.at[c, 1], to_x).start()
+
+    def x_far(c):
+        arrived(half_of(c, xh, op_z, 0), r_gf.at[c, 0])
+        arrived(half_of(c, xh, op_z, 1), r_gf.at[c, 1])
+        far = block_of(c, xh, op_z)
+        remote(far, far, c, r_gz.at[c], to_x).start()
+
+    def x_last(c):
+        arrived(block_of(c, 1 - xh, z), r_gx.at[c])
+        arrived(block_of(c, 1 - xh, dn_z), r_gp.at[c, 0])
+        arrived(block_of(c, 1 - xh, up_z), r_gp.at[c, 1])
+        arrived(block_of(c, 1 - xh, op_z), r_gz.at[c])
+
+    def either(z_step, x_step):
+        def step(c):
+            is_x = lax.rem(c, X_EVERY) == X_AT
+
+            @pl.when(is_x)
+            def _():
+                x_step(c)
+
+            @pl.when(jnp.logical_not(is_x))
+            def _():
+                z_step(c)
+
+        return step
 
     def up_form(c):
         w_all = w_v[c].reshape(N_ISL * RB, W)
@@ -248,36 +341,37 @@
             for step in steps:
                 step(c)
 
-    @pl.loop(0, n_chunk + LAG)
+    @pl.loop(0, n_chunk + LAG_F)
     def _(t):
-        def first(c):
+        def ahead(c):
             dup_form(c)
             dup_send(c)
 
-        at(t + 3, 0, n_chunk, first)
+        at(t + 3, 0, n_chunk, ahead)
         at(t + 1, 0, n_chunk, dup_share)
 
-        def second(c):
+        def start_sum(c):
             w_copy(c).wait()
             inner_form(c)
+            either(z_first, x_first)(c)
             up_form(c)
 
-        at(t, 0, n_chunk, second)
-        at(t - 1, 0, n_chunk, rs_second)
-        at(t - 2, 0, n_chunk, rs_x)
-
-        @pl.when(t == 3)
+        at(t, 0, n_chunk, start_sum)
+        at(t - LAG_A, 0, n_chunk, either(z_second, x_second))
+        at(t - LAG_B, 0, n_chunk, either(z_third, x_third))
+
+        @pl.when(t == LAG_C)
         def _():
             in_copies[4].wait()
             in_copies[5].wait()
 
-        at(t - 3, 0, n_chunk, update)
-        at(t - 4, 0, n_chunk, ag_partner)
-        at(t - 5, 0, n_chunk, ag_forward)
+        at(t - LAG_C, 0, n_chunk, either(z_update, x_update))
+        at(t - LAG_D, 0, n_chunk, either(z_partner, x_neighbours))
+        at(t - LAG_E, 0, n_chunk, either(z_forward, x_far))
         at(t, 0, n_chunk, ig_form)
-        at(t - 2, 0, n_chunk, up_add)
-        at(t - 5, 0, n_chunk, up_last)
-        at(t - 6, 0, n_chunk, ag_last)
+        at(t - LAG_UA, 0, n_chunk, up_add)
+        at(t - LAG_UB, 0, n_chunk, up_last)
+        at(t - LAG_F, 0, n_chunk, either(z_last, x_last))
 
     for half in range(2):
         ig_out[:, half] = acc_v[half * PLANE * TB : (half + 1) * PLANE * TB].astype(BF16).reshape(
@@ -301,11 +395,11 @@
     ig, gg, nw, no, nm = pl.pallas_call(
         functools.partial(kernel, c),
         out_shape=(
-            jax.ShapeDtypeStruct((PLANE, 2, TB, d_loc), BF16),
-            jax.ShapeDtypeStruct((TB, fs), BF16),
-            jax.ShapeDtypeStruct((N_ISL, RB, fs), BF16),
-            jax.ShapeDtypeStruct((RB, fs), F32),
-            jax.ShapeDtypeStruct((RB, fs), F32),
+            pltpu.VMEM((PLANE, 2, TB, d_loc), BF16),
+            pltpu.VMEM((TB, fs), BF16),
+            pltpu.VMEM((N_ISL, RB, fs), BF16),
+            pltpu.VMEM((RB, fs), F32),
+            pltpu.VMEM((RB, fs), F32),
         ),
         in_specs=[hbm] * 6,
         out_specs=(vmem,) * 5,
@@ -323,6 +417,7 @@
             pltpu.VMEM((c, 2, 2, RB, W), BF16),
             pltpu.VMEM((c, RB, W), BF16),
             pltpu.VMEM((c, RB, W), BF16),
+            pltpu.VMEM((-(-c // X_EVERY), N_Z, RB, W), BF16),
             pltpu.VMEM((c, PLANE * TB, W), BF16),
             pltpu.VMEM((c, PLANE * TB, W), BF16),
             pltpu.VMEM((c, PLANE * TB, W), BF16),
@@ -342,6 +437,7 @@
             dma((c, 2)),
             dma((c, 2)),
             dma((c, 2)),
+            dma((c,)),
             dma((c,)),
             dma((c,)),
         ],

time: 146 us -> 132 us (0.904)
  Pallas kernels: 132 us -> 124 us
  local copies, waits for them, and re-layouts: 13.4 us -> 6.9 us
    pallas_call x1, Pallas kernels: 132 us -> 124 us  [local(): pl.pallas_call(functools.partial(kernel, c), out_shape=(pltpu.VMEM((PLANE...]
    unnamed x11 -> x5, local copies, waits for them, and re-layouts: 13.4 us -> 6.9 us
where the time goes in v3:
time: 132 us
  Pallas kernels  124 us (94%)
  local copies, waits for them, and re-layouts  6.9 us (5%)
    pallas_call x1, Pallas kernels, local(): pl.pallas_call(functools.partial(kernel, c), out_shape=(pltpu.VMEM((PLANE...  124 us
    unnamed x5, local copies, waits for them, and re-layouts  6.9 us

profile of v3, /device:TPU:0, one launch (start us, length us, event | category | flops | bytes accessed | tf_op | source)
XLA Modules:
  0.0 131.8 jit_solution(7846231674631214163)
XLA Ops:
  0.6 124.3 %shard_map.101 = (bf16[8,2,32,1024]{3,2,1,0:T(8,128)(2,1)S(1)}, bf16[32,3328]{1,0:T(8,128)(2,1)S(1)}, bf16[8,128,3328]{2,1,0:T(8,128)(2,1)S(1)}, f32[128,3328]{1,0:T(8,128)S(1)}, f32[128,3328]{1,0:T(8,128)S(1)}) custom-call(bf16[8,2,32,1024]{3,2,1,0:T(8,128)(2,1)} %bitcast.11, bf16[32,3328]{1,0:T(8,128)(2,1)} %bitcast.12, bf16[32,3328]{1,0:T(8,128)(2,1)} %bitcast.13, ...), custom_call_target="tpu_custom_call" | custom-call | flops 10468982784 | bytes 27262976 | tf_op jit(solution)/shard_map/pallas_call | solution.py:395
  124.9 1.0 copy.16
  125.9 0.7 copy.17
  126.6 1.2 copy.19
  127.8 1.2 copy.20
  128.9 2.9 %copy.18 = bf16[1024,3328]{1,0:T(8,128)(2,1)} copy(bf16[1024,3328]{1,0:T(8,128)(2,1)S(1)} %bitcast.7) | data formatting | bytes 13631488

commit v4 on v3

--- a/solution.py
+++ b/solution.py
@@ -18,13 +18,15 @@
 W = 256
 N_Z = 4
 N_ISL = 8
+N_Y = 4
 PLANE = 8
 TB = 32
 RB = 128
 HB = RB // 2
-X_EVERY, X_AT = 4, 1
-LAG_A, LAG_B, LAG_C, LAG_D, LAG_E, LAG_F = 1, 2, 3, 4, 5, 6
-LAG_UA, LAG_UB = 2, 5
+X_CHUNKS = (0, 4, 6, 9, 11)
+LAG_A, LAG_B, LAG_C, LAG_D, LAG_E, LAG_F = 2, 4, 6, 10, 14, 18
+LAG_UA, LAG_UB, LAG_UC = 6, 9, 14
+AHEAD_B, AHEAD_C = 2, 1
 
 
 def kernel(
@@ -33,14 +35,16 @@
     ig_out, gg_out, nw_out, no_out, nm_out,
     x_v, xt_v, gate_v, cot_v, outer_v, mom_v, w_v, dup_v,
     inner_v, r1_v, r2_v, xs_v, rx_v, rxx_v,
-    ups_v, upr_v, upo_v, upt_v, upp_v, acc_v,
-    in_sem, w_sem, snd, r_dup, r_sib, r_s1, r_raw, r_acc, r_x,
-    r_gx, r_go, r_gp, r_gf, r_gz, r_ups, r_upp,
+    ups_v, upr_v, upo_v, upt_v, upp_v, upx_v, upy_v, acc_v,
+    in_sem, w_sem, snd, r_dup, r_dx, r_sib, r_s1, r_raw, r_acc, r_x,
+    r_gx, r_go, r_gp, r_gf, r_gz, r_ups, r_upp, r_upx,
 ):
     sec = lax.axis_index("section")
     isl = lax.axis_index("island")
     core = lax.rem(sec, 2)
     place = sec // 2
+    xl = place // N_Y
+    y = lax.rem(place, N_Y)
     z = lax.rem(isl, N_Z)
     xh = isl // N_Z
     up_z = lax.rem(z + 1, N_Z)
@@ -51,8 +55,13 @@
     to_x = (sec, (1 - xh) * N_Z + z)
     to_sib = (place * 2 + 1 - core, isl)
 
-    def peer(k):
-        return (lax.rem(place + k, PLANE) * 2 + core, isl)
+    to_xl = (((1 - xl) * N_Y + y) * 2 + core, isl)
+
+    def along_y(k):
+        return lax.rem(y + k, N_Y)
+
+    def peer(x_at, y_at):
+        return ((x_at * N_Y + y_at) * 2 + core, isl)
 
     def remote(src, dst, c, recv, device):
         return pltpu.make_async_remote_copy(
@@ -63,14 +72,17 @@
     def arrived(dst, recv):
         pltpu.make_async_copy(dst, dst, recv).wait()
 
+    def x_slot(c):
+        return sum((c > k).astype(jnp.int32) for k in X_CHUNKS)
+
     def cols(c):
         return pl.ds(pl.multiple_of(c * W, W), W)
 
     barrier = pltpu.get_barrier_semaphore()
-    for device in (to_up, to_dn, to_x, to_sib):
+    others = [(xl, along_y(k)) for k in (1, 2, 3)]
+    others += [(1 - xl, along_y(k)) for k in (0, 1, 2, 3)]
+    for device in [peer(*other) for other in others] + [to_sib, to_up, to_dn, to_x]:
         pl.semaphore_signal(barrier, inc=1, device_id=device, device_id_type=MESH)
-    for k in range(1, PLANE):
-        pl.semaphore_signal(barrier, inc=1, device_id=peer(k), device_id_type=MESH)
 
     def w_copy(c):
         return pltpu.make_async_copy(w_hbm.at[:, :, cols(c)], w_v.at[c], w_sem.at[c])
@@ -92,13 +104,29 @@
         d = cot_v[:, cols(c)].astype(F32) * g * s
         dup_v[c * 16 + core * PLANE + place] = d.astype(BF16)
 
+    def dup_at(c, p):
+        return dup_v.at[c * 16 + core * PLANE + p]
+
+    def dup_send_all(c):
+        mine = dup_at(c, place)
+        for other in others:
+            recv = r_dx.at[c] if other is others[3] else r_dup.at[c]
+            remote(mine, mine, c, recv, peer(*other)).start()
+
     def dup_send(c):
-        mine = dup_v.at[c * 16 + core * PLANE + place]
-        for k in range(1, PLANE):
-            remote(mine, mine, c, r_dup.at[c], peer(k)).start()
+        mine = dup_at(c, place)
+        remote(mine, mine, c, r_dx.at[c], to_xl).start()
+        for other in others[:3]:
+            remote(mine, mine, c, r_dup.at[c], peer(*other)).start()
+
+    def dup_pass(c):
+        theirs = dup_at(c, (1 - xl) * N_Y + y)
+        arrived(theirs, r_dx.at[c])
+        for other in others[:3]:
+            remote(theirs, theirs, c, r_dup.at[c], peer(*other)).start()
 
     def dup_share(c):
-        arrived(dup_v.at[pl.ds(c * 16 + core * PLANE, PLANE - 1)], r_dup.at[c])
+        arrived(dup_v.at[pl.ds(c * 16 + core * PLANE, PLANE - 2)], r_dup.at[c])
         half = dup_v.at[pl.ds(c * 16 + core * PLANE, PLANE)]
         remote(half, half, c, r_sib.at[c], to_sib).start()
 
@@ -145,10 +173,10 @@
         remote(xs_v.at[c], rx_v.at[c], c, r_x.at[c], to_x).start()
 
     def x_first(c):
-        remote(inner_v.at[c, 1 - xh], rxx_v.at[c // X_EVERY], c, r_x.at[c], to_x).start()
+        remote(inner_v.at[c, 1 - xh], rxx_v.at[x_slot(c)], c, r_x.at[c], to_x).start()
 
     def x_second(c):
-        got = rxx_v.at[c // X_EVERY]
+        got = rxx_v.at[x_slot(c)]
         arrived(got, r_x.at[c])
         low, high = pl.ds(0, HB), pl.ds(HB, HB)
         far, above, below = (inner_v.at[c, xh, rel] for rel in (2, 1, 3))
@@ -206,7 +234,7 @@
         update(
             c,
             inner_v[c, xh, 0].astype(F32)
-            + rxx_v[c // X_EVERY, 0].astype(F32)
+            + rxx_v[x_slot(c), 0].astype(F32)
             + r2_v[c, 0, 0].astype(F32)
             + r2_v[c, 1, 0].astype(F32),
         )
@@ -260,7 +288,7 @@
 
     def either(z_step, x_step):
         def step(c):
-            is_x = lax.rem(c, X_EVERY) == X_AT
+            is_x = functools.reduce(jnp.logical_or, [c == k for k in X_CHUNKS])
 
             @pl.when(is_x)
             def _():
@@ -283,18 +311,24 @@
     def up_add(c):
         arrived(upr_v.at[c], r_ups.at[c])
         both = upo_v[c].astype(F32) + upr_v[c].astype(F32)
-        upt_v[pl.ds(c * PLANE, PLANE)] = both.astype(BF16).reshape(PLANE, TB, W)
-        for k in range(1, PLANE):
-            to = lax.rem(place + k, PLANE)
+        upt_v[c] = both.astype(BF16).reshape(2, N_Y, TB, W)
+        for k in (1, 2, 3):
+            to = along_y(k)
             remote(
-                upt_v.at[c * PLANE + to], upp_v.at[c * PLANE + place], c, r_upp.at[c], peer(k)
+                upt_v.at[c, :, to], upp_v.at[c, y], c, r_upp.at[c], peer(xl, to)
             ).start()
 
+    def up_cross(c):
+        arrived(upp_v.at[c, pl.ds(0, N_Y - 1)], r_upp.at[c])
+        total = upt_v[c, :, y].astype(F32)
+        for k in (1, 2, 3):
+            total = total + upp_v[c, along_y(k)].astype(F32)
+        upy_v[c] = total.astype(BF16)
+        remote(upy_v.at[c, 1 - xl], upx_v.at[c], c, r_upx.at[c], to_xl).start()
+
     def up_last(c):
-        arrived(upp_v.at[pl.ds(c * PLANE, PLANE - 1)], r_upp.at[c])
-        up = upt_v[c * PLANE + place].astype(F32)
-        for k in range(1, PLANE):
-            up = up + upp_v[c * PLANE + lax.rem(place + k, PLANE)].astype(F32)
+        arrived(upx_v.at[c], r_upx.at[c])
+        up = upy_v[c, xl].astype(F32) + upx_v[c].astype(F32)
         g = gate_v[:, cols(c)].astype(F32)
         s = jax.nn.sigmoid(g)
         out = cot_v[:, cols(c)].astype(F32) * up * s * (1.0 + g * (1.0 - s))
@@ -310,30 +344,38 @@
 
     in_copies[0].wait()
     in_copies[1].wait()
-    w_copy(0).start()
-    dup_form(0)
-    pl.semaphore_wait(barrier, 3 + PLANE)
-    dup_send(0)
-
-    @pl.loop(1, 3)
+    @pl.loop(0, n_chunk)
     def _(c):
         dup_form(c)
-        dup_send(c)
+
+    pl.semaphore_wait(barrier, 4 + PLANE - 1)
+    dup_send_all(0)
 
     @pl.loop(1, n_chunk)
     def _(c):
-        w_copy(c).start()
-
-    in_copies[4].start()
-    in_copies[5].start()
+        dup_send(c)
+
+    w_copy(0).start()
     in_copies[2].wait()
     in_copies[3].wait()
     for block in range(N_ISL):
         piece = x_v[:, :, :, block * RB : (block + 1) * RB].reshape(16 * TB, RB)
         rel = lax.rem(block % N_Z + N_Z - z, N_Z)
         xt_v[block // N_Z, rel] = piece.T
+    arrived(dup_at(0, (1 - xl) * N_Y + y), r_dx.at[0])
+    dup_share(0)
+
+    @pl.loop(1, n_chunk)
+    def _(c):
+        w_copy(c).start()
+
+    @pl.loop(1, AHEAD_B)
+    def _(c):
+        dup_pass(c)
+
+    in_copies[4].start()
+    in_copies[5].start()
     acc_v[...] = jnp.zeros_like(acc_v)
-    dup_share(0)
 
     def at(c, lo, hi, *steps):
         @pl.when((c >= lo) & (c < hi))
@@ -343,13 +385,6 @@
 
     @pl.loop(0, n_chunk + LAG_F)
     def _(t):
-        def ahead(c):
-            dup_form(c)
-            dup_send(c)
-
-        at(t + 3, 0, n_chunk, ahead)
-        at(t + 1, 0, n_chunk, dup_share)
-
         def start_sum(c):
             w_copy(c).wait()
             inner_form(c)
@@ -357,6 +392,9 @@
             up_form(c)
 
         at(t, 0, n_chunk, start_sum)
+
+        at(t + AHEAD_B, 0, n_chunk, dup_pass)
+        at(t + AHEAD_C, 0, n_chunk, dup_share)
         at(t - LAG_A, 0, n_chunk, either(z_second, x_second))
         at(t - LAG_B, 0, n_chunk, either(z_third, x_third))
 
@@ -369,14 +407,17 @@
         at(t - LAG_D, 0, n_chunk, either(z_partner, x_neighbours))
         at(t - LAG_E, 0, n_chunk, either(z_forward, x_far))
         at(t, 0, n_chunk, ig_form)
+
+        @pl.when(t == n_chunk + LAG_A)
+        def _():
+            for half in range(2):
+                rows = acc_v[half * PLANE * TB : (half + 1) * PLANE * TB].astype(BF16)
+                ig_out[:, half] = rows.reshape(PLANE, TB, N_ISL * RB)
+
         at(t - LAG_UA, 0, n_chunk, up_add)
-        at(t - LAG_UB, 0, n_chunk, up_last)
+        at(t - LAG_UB, 0, n_chunk, up_cross)
+        at(t - LAG_UC, 0, n_chunk, up_last)
         at(t - LAG_F, 0, n_chunk, either(z_last, x_last))
-
-    for half in range(2):
-        ig_out[:, half] = acc_v[half * PLANE * TB : (half + 1) * PLANE * TB].astype(BF16).reshape(
-            PLANE, TB, N_ISL * RB
-        )
 
     sent = (2 * 7 * TB + 2 * PLANE * TB + 6 * RB + RB + 3 * RB + 2 * RB + 2 * RB) // TB
 
@@ -417,14 +458,17 @@
             pltpu.VMEM((c, 2, 2, RB, W), BF16),
             pltpu.VMEM((c, RB, W), BF16),
             pltpu.VMEM((c, RB, W), BF16),
-            pltpu.VMEM((-(-c // X_EVERY), N_Z, RB, W), BF16),
+            pltpu.VMEM((len(X_CHUNKS), N_Z, RB, W), BF16),
             pltpu.VMEM((c, PLANE * TB, W), BF16),
             pltpu.VMEM((c, PLANE * TB, W), BF16),
             pltpu.VMEM((c, PLANE * TB, W), BF16),
-            pltpu.VMEM((c * PLANE, TB, W), BF16),
-            pltpu.VMEM((c * PLANE, TB, W), BF16),
+            pltpu.VMEM((c, 2, N_Y, TB, W), BF16),
+            pltpu.VMEM((c, N_Y, 2, TB, W), BF16),
+            pltpu.VMEM((c, TB, W), BF16),
+            pltpu.VMEM((c, 2, TB, W), BF16),
             pltpu.VMEM((tok, d_loc), F32),
             dma((6,)),
+            dma((c,)),
             dma((c,)),
             dma((c,)),
             dma((c,)),
@@ -437,6 +481,7 @@
             dma((c, 2)),
             dma((c, 2)),
             dma((c, 2)),
+            dma((c,)),
             dma((c,)),
             dma((c,)),
             dma((c,)),

time: 132 us -> 124 us (0.939)
  Pallas kernels: 124 us -> 116 us
    pallas_call x1, Pallas kernels: 124 us -> 116 us  [local(): pl.pallas_call(functools.partial(kernel, c), out_shape=(pltpu.VMEM((PLANE...]
where the time goes in v4:
time: 124 us; the launch traced here: 123 us
  Pallas kernels  116 us (94%)
  local copies, waits for them, and re-layouts  6.9 us (6%)
    pallas_call x1, Pallas kernels, local(): pl.pallas_call(functools.partial(kernel, c), out_shape=(pltpu.VMEM((PLANE...  116 us
    unnamed x5, local copies, waits for them, and re-layouts  6.9 us

profile of v4, /device:TPU:0, one launch (start us, length us, event | category | flops | bytes accessed | tf_op | source)
XLA Modules:
  0.0 123.1 jit_solution(15427992126704830181)
XLA Ops:
  0.6 115.6 %shard_map.101 = (bf16[8,2,32,1024]{3,2,1,0:T(8,128)(2,1)S(1)}, bf16[32,3328]{1,0:T(8,128)(2,1)S(1)}, bf16[8,128,3328]{2,1,0:T(8,128)(2,1)S(1)}, f32[128,3328]{1,0:T(8,128)S(1)}, f32[128,3328]{1,0:T(8,128)S(1)}) custom-call(bf16[8,2,32,1024]{3,2,1,0:T(8,128)(2,1)} %bitcast.11, bf16[32,3328]{1,0:T(8,128)(2,1)} %bitcast.12, bf16[32,3328]{1,0:T(8,128)(2,1)} %bitcast.13, ...), custom_call_target="tpu_custom_call" | custom-call | flops 10468982784 | bytes 27262976 | tf_op jit(solution)/shard_map/pallas_call | solution.py:436
  116.2 1.0 copy.16
  117.2 0.7 copy.17
  117.9 1.2 copy.19
  119.1 1.2 copy.20
  120.3 2.9 %copy.18 = bf16[1024,3328]{1,0:T(8,128)(2,1)} copy(bf16[1024,3328]{1,0:T(8,128)(2,1)S(1)} %bitcast.7) | data formatting | bytes 13631488

commit v5 on v4

--- a/solution.py
+++ b/solution.py
@@ -27,6 +27,7 @@
 LAG_A, LAG_B, LAG_C, LAG_D, LAG_E, LAG_F = 2, 4, 6, 10, 14, 18
 LAG_UA, LAG_UB, LAG_UC = 6, 9, 14
 AHEAD_B, AHEAD_C = 2, 1
+FIRST = 3
 
 
 def kernel(
@@ -200,7 +201,7 @@
         remote(below, r2_v.at[c, 1, 0, high], c, r_acc.at[c, 1], to_dn).start()
 
     def block_of(c, half, zz):
-        return nw_out.at[half * N_Z + zz, :, cols(c)]
+        return nw_out.at[c, half * N_Z + zz]
 
     def update(c, total):
         own = outer_v[:, cols(c)]
@@ -209,7 +210,7 @@
         new = own - outer_rate * (delta + nesterov_mu * moment)
         nm_out[:, cols(c)] = moment
         no_out[:, cols(c)] = new
-        nw_out[isl, :, cols(c)] = new.astype(BF16)
+        nw_out[c, isl] = new.astype(BF16)
         mine = block_of(c, xh, z)
         remote(mine, mine, c, r_gx.at[c], to_x).start()
         remote(mine, mine, c, r_go.at[c, 0], to_up).start()
@@ -260,7 +261,7 @@
         arrived(block_of(c, 1, op_z), r_gf.at[c, 1])
 
     def half_of(c, half, zz, part):
-        return nw_out.at[half * N_Z + zz, pl.ds(part * HB, HB), cols(c)]
+        return nw_out.at[c, half * N_Z + zz, pl.ds(part * HB, HB)]
 
     def x_neighbours(c):
         below = block_of(c, xh, dn_z)
@@ -349,9 +350,10 @@
         dup_form(c)
 
     pl.semaphore_wait(barrier, 4 + PLANE - 1)
-    dup_send_all(0)
-
-    @pl.loop(1, n_chunk)
+    for c in range(FIRST):
+        dup_send_all(c)
+
+    @pl.loop(FIRST, n_chunk)
     def _(c):
         dup_send(c)
 
@@ -362,14 +364,15 @@
         piece = x_v[:, :, :, block * RB : (block + 1) * RB].reshape(16 * TB, RB)
         rel = lax.rem(block % N_Z + N_Z - z, N_Z)
         xt_v[block // N_Z, rel] = piece.T
-    arrived(dup_at(0, (1 - xl) * N_Y + y), r_dx.at[0])
-    dup_share(0)
+    for c in range(FIRST):
+        arrived(dup_at(c, (1 - xl) * N_Y + y), r_dx.at[c])
+        dup_share(c)
 
     @pl.loop(1, n_chunk)
     def _(c):
         w_copy(c).start()
 
-    @pl.loop(1, AHEAD_B)
+    @pl.loop(FIRST, max(FIRST, AHEAD_B))
     def _(c):
         dup_pass(c)
 
@@ -393,8 +396,8 @@
 
         at(t, 0, n_chunk, start_sum)
 
-        at(t + AHEAD_B, 0, n_chunk, dup_pass)
-        at(t + AHEAD_C, 0, n_chunk, dup_share)
+        at(t + AHEAD_B, max(FIRST, AHEAD_B), n_chunk, dup_pass)
+        at(t + AHEAD_C, FIRST, n_chunk, dup_share)
         at(t - LAG_A, 0, n_chunk, either(z_second, x_second))
         at(t - LAG_B, 0, n_chunk, either(z_third, x_third))
 
@@ -424,6 +427,18 @@
     @pl.loop(0, n_chunk)
     def _(c):
         arrived(dup_v.at[pl.ds(0, sent)], snd.at[c])
+
+
+def write_out(ig, gg, nw, no, nm, ig_out, gg_out, nw_out, no_out, nm_out, sem):
+    pairs = [(nw.at[c], nw_out.at[:, :, c * W : (c + 1) * W]) for c in range(nw.shape[0])]
+    pairs += [(no, no_out), (nm, nm_out), (ig, ig_out), (gg, gg_out)]
+    copies = [
+        pltpu.make_async_copy(src, dst, sem.at[k]) for k, (src, dst) in enumerate(pairs)
+    ]
+    for copy in copies:
+        copy.start()
+    for copy in copies:
+        copy.wait()
 
 
 def local(inputs, gate_pre, up_cot, weights, outer, momentum):
@@ -433,12 +448,12 @@
     dma = pltpu.SemaphoreType.DMA
     vmem = pl.BlockSpec(memory_space=pltpu.VMEM)
     hbm = pl.BlockSpec(memory_space=pltpu.HBM)
-    ig, gg, nw, no, nm = pl.pallas_call(
+    results = pl.pallas_call(
         functools.partial(kernel, c),
         out_shape=(
             pltpu.VMEM((PLANE, 2, TB, d_loc), BF16),
             pltpu.VMEM((TB, fs), BF16),
-            pltpu.VMEM((N_ISL, RB, fs), BF16),
+            pltpu.VMEM((c, N_ISL, RB, W), BF16),
             pltpu.VMEM((RB, fs), F32),
             pltpu.VMEM((RB, fs), F32),
         ),
@@ -500,6 +515,20 @@
         outer,
         momentum,
     )
+    ig, gg, nw, no, nm = pl.pallas_call(
+        write_out,
+        out_shape=(
+            jax.ShapeDtypeStruct((PLANE, 2, TB, d_loc), BF16),
+            jax.ShapeDtypeStruct((TB, fs), BF16),
+            jax.ShapeDtypeStruct((N_ISL, RB, fs), BF16),
+            jax.ShapeDtypeStruct((RB, fs), F32),
+            jax.ShapeDtypeStruct((RB, fs), F32),
+        ),
+        in_specs=[vmem] * 5,
+        out_specs=(hbm,) * 5,
+        scratch_shapes=[dma((c + 4,))],
+        compiler_params=pltpu.CompilerParams(vmem_limit_bytes=2 * 2**20),
+    )(*results)
     return (
         ig.reshape(1, tok, d_loc),
         gg[None],

time: 124 us -> 116 us (0.935)
  local copies, waits for them, and re-layouts: 6.9 us -> 0 us
    unnamed x5 -> x0, local copies, waits for them, and re-layouts: 6.9 us -> none
    pallas_call x1, Pallas kernels: 116 us -> 111 us  [local(): pl.pallas_call(functools.partial(kernel, c), out_shape=(pltpu.VMEM((PLANE...]
    pallas_call x0 -> x1, Pallas kernels: none -> 4.34 us  [local(): pl.pallas_call(write_out, out_shape=(jax.ShapeDtypeStruct((PLANE, 2, TB,...]
where the time goes in v5:
time: 116 us
  Pallas kernels  115 us (99%)
    pallas_call x1, Pallas kernels, local(): pl.pallas_call(functools.partial(kernel, c), out_shape=(pltpu.VMEM((PLANE...  111 us
    pallas_call x1, Pallas kernels, local(): pl.pallas_call(write_out, out_shape=(jax.ShapeDtypeStruct((PLANE, 2, TB,...  4.34 us

profile of v5, /device:TPU:0, one launch (start us, length us, event | category | flops | bytes accessed | tf_op | source)
XLA Modules:
  0.0 116.1 jit_solution(15064745831974865178)
XLA Ops:
  0.6 111.1 %shard_map.101 = (bf16[8,2,32,1024]{3,2,1,0:T(8,128)(2,1)S(1)}, bf16[32,3328]{1,0:T(8,128)(2,1)S(1)}, bf16[13,8,128,256]{3,2,1,0:T(8,128)(2,1)S(1)}, f32[128,3328]{1,0:T(8,128)S(1)}, f32[128,3328]{1,0:T(8,128)S(1)}) custom-call(bf16[8,2,32,1024]{3,2,1,0:T(8,128)(2,1)} %bitcast.9, bf16[32,3328]{1,0:T(8,128)(2,1)} %bitcast.11, bf16[32,3328]{1,0:T(8,128)(2,1)} %bitcast.12, ...), custom_call_target="tpu_custom_call" | custom-call | flops 10468982784 | bytes 27262976 | tf_op jit(solution)/shard_map/pallas_call | solution.py:451
  111.7 4.3 %shard_map.102 = (bf16[8,2,32,1024]{3,2,1,0:T(8,128)(2,1)}, bf16[32,3328]{1,0:T(8,128)(2,1)}, bf16[8,128,3328]{2,1,0:T(8,128)(2,1)}, f32[128,3328]{1,0:T(8,128)}, f32[128,3328]{1,0:T(8,128)}) custom-call(bf16[8,2,32,1024]{3,2,1,0:T(8,128)(2,1)S(1)} %get-tuple-element.15.ig, bf16[32,3328]{1,0:T(8,128)(2,1)S(1)} %get-tuple-element.16.gg, ...), custom_call_target="tpu_custom_call" | custom-call | tf_op jit(solution)/shard_map/pallas_call | solution.py:518

commit v6 on v5

--- a/solution.py
+++ b/solution.py
@@ -23,11 +23,12 @@
 TB = 32
 RB = 128
 HB = RB // 2
-X_CHUNKS = (0, 4, 6, 9, 11)
+X_CHUNKS = (1, 4, 6, 9, 11)
 LAG_A, LAG_B, LAG_C, LAG_D, LAG_E, LAG_F = 2, 4, 6, 10, 14, 18
 LAG_UA, LAG_UB, LAG_UC = 6, 9, 14
 AHEAD_B, AHEAD_C = 2, 1
 FIRST = 3
+EARLY = 2
 
 
 def kernel(
@@ -364,9 +365,12 @@
         piece = x_v[:, :, :, block * RB : (block + 1) * RB].reshape(16 * TB, RB)
         rel = lax.rem(block % N_Z + N_Z - z, N_Z)
         xt_v[block // N_Z, rel] = piece.T
-    for c in range(FIRST):
+    def share_first(c):
         arrived(dup_at(c, (1 - xl) * N_Y + y), r_dx.at[c])
         dup_share(c)
+
+    for c in range(EARLY):
+        share_first(c)
 
     @pl.loop(1, n_chunk)
     def _(c):
@@ -397,6 +401,7 @@
         at(t, 0, n_chunk, start_sum)
 
         at(t + AHEAD_B, max(FIRST, AHEAD_B), n_chunk, dup_pass)
+        at(t + AHEAD_C, EARLY, FIRST, share_first)
         at(t + AHEAD_C, FIRST, n_chunk, dup_share)
         at(t - LAG_A, 0, n_chunk, either(z_second, x_second))
         at(t - LAG_B, 0, n_chunk, either(z_third, x_third))

time: 116 us -> 115 us (level)
    pallas_call x1, Pallas kernels: 111 us -> 110 us  [local(): pl.pallas_call(functools.partial(kernel, c), out_shape=(pltpu.VMEM((PLANE...]
where the time goes in v6:
time: 115 us
  Pallas kernels  114 us (99%)
    pallas_call x1, Pallas kernels, local(): pl.pallas_call(functools.partial(kernel, c), out_shape=(pltpu.VMEM((PLANE...  110 us
    pallas_call x1, Pallas kernels, local(): pl.pallas_call(write_out, out_shape=(jax.ShapeDtypeStruct((PLANE, 2, TB,...  4.34 us

profile of v6, /device:TPU:0, one launch (start us, length us, event | category | flops | bytes accessed | tf_op | source)
XLA Modules:
  0.0 114.7 jit_solution(12650851996843344693)
XLA Ops:
  0.6 109.7 %shard_map.101 = (bf16[8,2,32,1024]{3,2,1,0:T(8,128)(2,1)S(1)}, bf16[32,3328]{1,0:T(8,128)(2,1)S(1)}, bf16[13,8,128,256]{3,2,1,0:T(8,128)(2,1)S(1)}, f32[128,3328]{1,0:T(8,128)S(1)}, f32[128,3328]{1,0:T(8,128)S(1)}) custom-call(bf16[8,2,32,1024]{3,2,1,0:T(8,128)(2,1)} %bitcast.9, bf16[32,3328]{1,0:T(8,128)(2,1)} %bitcast.11, bf16[32,3328]{1,0:T(8,128)(2,1)} %bitcast.12, ...), custom_call_target="tpu_custom_call" | custom-call | flops 10468982784 | bytes 27262976 | tf_op jit(solution)/shard_map/pallas_call | solution.py:456
  110.4 4.3 %shard_map.102 = (bf16[8,2,32,1024]{3,2,1,0:T(8,128)(2,1)}, bf16[32,3328]{1,0:T(8,128)(2,1)}, bf16[8,128,3328]{2,1,0:T(8,128)(2,1)}, f32[128,3328]{1,0:T(8,128)}, f32[128,3328]{1,0:T(8,128)}) custom-call(bf16[8,2,32,1024]{3,2,1,0:T(8,128)(2,1)S(1)} %get-tuple-element.15.ig, bf16[32,3328]{1,0:T(8,128)(2,1)S(1)} %get-tuple-element.16.gg, ...), custom_call_target="tpu_custom_call" | custom-call | tf_op jit(solution)/shard_map/pallas_call | solution.py:523
